TPU v7x, 256 devices: a whole 4x4x8 slice. The times are simulated.
256 devices in a mesh: vox: 8 (over x, core), mem: 32 (over y, z).
Axes of the slice: x: 4, y: 4, z: 8, core: 2. Of those that a mesh axis runs over, the one named last changes fastest.
Arguments:
- ensemble: bfloat16 [256, 524288], P('mem', 'vox'), may hold values from -6 to 6
- partials: float32 [8, 256, 131072], P('vox', 'mem'), may hold values from -6 to 6
- perturb: float32 [256, 131072], P('mem', 'vox'), may hold values from -6 to 6
- observed: float32 [131072], P('vox'), may hold values from -6 to 6
- variance: float32 [131072], P('vox'), may hold values from 0.5 to 2
- obs_lists: int32 [4096, 64], P(('vox', 'mem')), may hold values from 0 to 127, all different within a row
- taper_index: int32 [4096, 64], P(('vox', 'mem')), may hold values from 0 to 15
- taper_table: float32 [16], replicated, may hold values from 0.1 to 1
Outputs:
- updated: bfloat16 [256, 524288], P('mem', 'vox')
All inputs are finite; a program needn't handle non-finite values.
Results may differ from a plain program's by a relative error of at most 0.017.
Values may be sent and summed in bfloat16 or wider, within the bound.
A program may use at most 128 MiB of HBM per device.

v0:
```python
import jax
import jax.numpy as jnp
from jax import lax
from jax.sharding import PartitionSpec as P

OB = 128


def center(values):
    as_float = values.astype(jnp.float32)
    return (as_float - jnp.mean(as_float, axis=0, keepdims=True)).astype(jnp.bfloat16)


def block_moments(obs_anom, weights):
    return jnp.einsum("kbi,lbi->bkl", obs_anom, weights, preferred_element_type=jnp.float32)


def from_moments(moments, coeff, state_anom):
    high = lax.Precision.HIGHEST
    combined = jnp.einsum("bo,okl->bkl", coeff, moments, precision=high).astype(jnp.bfloat16)
    return jnp.einsum("kbc,bkl->lbc", state_anom, combined, preferred_element_type=jnp.float32)


def local(ensemble, partials, perturb, observed, variance, obs_lists, taper_index, taper_table):
    summed = lax.psum_scatter(
        partials[0].astype(jnp.bfloat16), "vox", scatter_dimension=1, tiled=True
    )
    weights = (
        (observed[None, :] + perturb - summed.astype(jnp.float32)) / variance[None, :]
    ).astype(jnp.bfloat16)
    members = lax.all_to_all(ensemble, "mem", split_axis=1, concat_axis=0, tiled=True)
    count = members.shape[0]
    blocks = obs_lists.shape[0]
    cells = members.shape[1] // blocks
    groups = weights.shape[1] // OB
    state_anom = center(members).reshape(count, blocks, cells)
    table_hits = (
        taper_index[:, :, None] == jnp.arange(taper_table.shape[0], dtype=jnp.int32)[None, None, :]
    ).astype(jnp.float32)
    tapers = jnp.sum(table_hits * taper_table[None, None, :], axis=2)
    picks = (obs_lists[:, :, None] == jnp.arange(groups, dtype=jnp.int32)[None, None, :]).astype(
        jnp.float32
    )
    coeff = jnp.sum(tapers[:, :, None] * picks, axis=1)
    pred_all, wts_all = (
        lax.all_gather(summed, "mem", axis=0, tiled=True),
        lax.all_gather(weights, "mem", axis=0, tiled=True),
    )
    obs_anom = center(pred_all).reshape(count, groups, OB)
    moments = block_moments(obs_anom, wts_all.reshape(count, groups, OB))
    increment = from_moments(moments, coeff, state_anom).reshape(count, blocks * cells)
    updated = (members.astype(jnp.float32) + increment * (1.0 / (count - 1))).astype(jnp.bfloat16)
    return lax.all_to_all(updated, "mem", split_axis=0, concat_axis=1, tiled=True)


def solution(mesh):
    return jax.shard_map(
        local,
        mesh=mesh,
        in_specs=(
            P("mem", "vox"),
            P("vox", "mem", None),
            P("mem", "vox"),
            P("vox"),
            P("vox"),
            P(("vox", "mem"), None),
            P(("vox", "mem"), None),
            P(),
        ),
        out_specs=P("mem", "vox"),
        check_vma=False,
    )
```

profile of v0, /device:TPU:2, one launch (start us, length us, event | category | flops | bytes accessed | tf_op | source)
XLA Modules:
  0.0 376.0 jit_solution(18339346806040277107)
XLA Ops:
  6.5 0.0 copy-start
  6.5 0.0 copy-start.2
  6.5 0.0 copy-start.1
  6.5 0.0 reduce-scatter.2.cloned.1.call-start
  6.5 3.8 %convert_bitcast_fusion.2 = bf16[8,131072]{1,0:T(8,128)(2,1)} fusion(f32[1,8,131072]{2,1,0:T(8,128)} %param.9), kind=kLoop, calls=%fused_computation.19 | loop fusion | flops 1048576 | bytes 6291456 | tf_op jit(solution)/shard_map/convert_element_type | solution.py:26
  10.3 0.0 copy-start.4
  10.3 0.0 copy-start.5
  10.3 0.0 copy-start.3
  10.3 0.0 reduce-scatter.2.cloned.1.call-update
  10.4 0.0 all-gather.3.cloned.1.call-start
  10.4 36.0 %reduce-scatter.2.cloned.1.call-done = bf16[8,16384]{1,0:T(8,128)(2,1)} async-done(((bf16[8,131072]{1,0:T(8,128)(2,1)}), bf16[8,16384]{1,0:T(8,128)(2,1)}) %reduce-scatter.2.cloned.1.call-update) | async-done | bytes 262160 | tf_op jit(solution)/shard_map/reduce_scatter | solution.py:25
  46.4 0.0 all-gather.3.cloned.1.call-update
  46.4 0.0 all-gather.5.cloned.1.call-start
  46.5 0.0 copy-done
  46.5 0.0 copy-done.2
  46.5 0.0 copy-done.1
  46.5 1.8 divide_convert_fusion
  48.3 0.0 all-gather.5.cloned.1.call-update
  48.3 9.8 %all-to-all-start = ((bf16[8,32,2048]{2,0,1:T(8,128)(2,1)}), bf16[8,32,2048]{2,0,1:T(8,128)(2,1)S(1)}, u32[]{:S(2)}, u32[]{:S(2)}) async-start(bf16[8,32,2048]{2,0,1:T(8,128)(2,1)} %bitcast), calls=%async_computation | async-start | bytes 2097152 | tf_op jit(solution)/shard_map/all_to_all | solution.py:31
  58.1 0.0 copy-done.4
  58.1 0.0 copy-done.5
  58.1 0.1 select_reduce_fusion.1
  58.2 0.0 copy-done.3
  58.2 0.3 select_reduce_fusion
  58.6 32.4 %all-to-all-done = bf16[8,32,2048]{2,0,1:T(8,128)(2,1)S(1)} async-done(((bf16[8,32,2048]{2,0,1:T(8,128)(2,1)}), bf16[8,32,2048]{2,0,1:T(8,128)(2,1)S(1)}, u32[]{:S(2)}, u32[]{:S(2)}) %all-to-all-start) | async-done | bytes 1048608 | tf_op jit(solution)/shard_map/all_to_all | solution.py:31
  91.0 0.2 convert_bitcast_fusion
  91.3 0.4 copy.36
  91.7 0.2 convert_reduce_fusion.1
  91.8 0.2 fusion.9
  92.0 65.0 %all-gather.3.cloned.1.call-done = bf16[256,16384]{1,0:T(8,128)(2,1)} async-done(((bf16[8,16384]{1,0:T(8,128)(2,1)}), bf16[256,16384]{1,0:T(8,128)(2,1)}) %all-gather.3.cloned.1.call-update) | async-done | bytes 8388624 | tf_op jit(solution)/shard_map/all_gather | solution.py:46
  157.0 4.8 %convert_reduce_fusion = f32[16384]{0:T(1024)S(1)} fusion(bf16[256,16384]{1,0:T(8,128)(2,1)} %all-gather.3.cloned.1.call-done), kind=kLoop, calls=%fused_computation.3 | loop fusion | flops 8372224 | bytes 8454144 | tf_op jit(solution)/shard_map/reduce_sum | solution.py:11
  161.8 93.4 %all-gather.5.cloned.1.call-done = bf16[256,16384]{1,0:T(8,128)(2,1)} async-done(((bf16[8,16384]{1,0:T(8,128)(2,1)}), bf16[256,16384]{1,0:T(8,128)(2,1)}) %all-gather.5.cloned.1.call-update) | async-done | bytes 8388624 | tf_op jit(solution)/shard_map/all_gather | solution.py:47
  255.2 11.9 %copy.27 = bf16[256,16384]{0,1:T(8,128)(2,1)} copy(bf16[256,16384]{1,0:T(8,128)(2,1)} %all-gather.5.cloned.1.call-done) | data formatting | bytes 16777216 | tf_op jit(solution)/shard_map/all_gather | solution.py:47
  267.2 17.8 %fusion.4 = f32[128,256,256]{2,1,0:T(8,128)} fusion(bf16[256,128,128]{0,2,1:T(8,128)(2,1)} %bitcast.35, bf16[256,16384]{1,0:T(8,128)(2,1)} %all-gather.3.cloned.1.call-done, f32[16384]{0:T(1024)S(1)} %broadcast_multiply_fusion), kind=kOutput, calls=%fused_computation.6 | convolution fusion | flops 2160066560 | bytes 50397184 | tf_op jit(solution)/shard_map/kbi,lbi->bkl/dot_general | solution.py:15
  284.9 43.5 %fusion.12 = bf16[16,256,256]{2,0,1:T(8,128)(2,1)S(1)} fusion(f32[128,256,256]{2,1,0:T(8,128)} %fusion.4, f32[16,128]{1,0:T(8,128)S(1)} %select_reduce_fusion), kind=kOutput, calls=%fused_computation.20 | convolution fusion | flops 1611661312 | bytes 35659776 | tf_op jit(solution)/shard_map/bo,okl->bkl/dot_general | solution.py:20
  328.5 1.7 multiply_bitcast_fusion
  330.1 2.6 copy.33
  332.7 1.7 mul.36
  334.4 0.3 fusion.8
  334.7 33.8 %all_to_all.29 = bf16[32,8,2048]{2,1,0:T(8,128)(2,1)S(1)} all-to-all(bf16[32,8,2048]{2,1,0:T(8,128)(2,1)S(1)} %fusion.8), channel_id=1, replica_groups=mesh['vox'=8,'mem'=32] {'mem'}, dimensions={0} | all-to-all | bytes 2097152 | tf_op jit(solution)/shard_map/all_to_all | solution.py:53
  368.5 1.0 copy.52
  (2 shorter events, 0.0 us)
Async XLA Ops:
  6.5 39.9 %copy-start = (f32[8,16384]{1,0:T(8,128)S(1)}, f32[8,16384]{1,0:T(8,128)}, u32[]{:S(2)}) copy-start(f32[8,16384]{1,0:T(8,128)} %param.10) | copy-start | bytes 1572868
  6.5 40.0 %copy-start.2 = (f32[16384]{0:T(1024)S(1)}, f32[16384]{0:T(1024)}, u32[]{:S(2)}) copy-start(f32[16384]{0:T(1024)} %param.11) | copy-start | bytes 196612
  6.5 40.0 %copy-start.1 = (f32[16384]{0:T(1024)S(1)}, f32[16384]{0:T(1024)}, u32[]{:S(2)}) copy-start(f32[16384]{0:T(1024)} %param.12) | copy-start | bytes 196612
  6.5 39.9 %reduce-scatter.2.cloned.1.call-start = ((), (), s32[]{:S(2)}) async-start(), calls=%async_computation.3 | async-start | bytes 2359296 | tf_op jit(solution)/shard_map/reduce_scatter | solution.py:25
  10.3 47.8 %copy-start.4 = (s32[16,64]{1,0:T(8,128)S(1)}, s32[16,64]{1,0:T(8,128)}, u32[]{:S(2)}) copy-start(s32[16,64]{1,0:T(8,128)} %param.14) | copy-start | bytes 12292
  10.3 47.8 %copy-start.5 = (f32[16]{0:T(128)S(1)}, f32[16]{0:T(128)}, u32[]{:S(2)}) copy-start(f32[16]{0:T(128)} %param.15) | copy-start | bytes 196
  10.3 47.9 %copy-start.3 = (s32[16,64]{1,0:T(8,128)S(1)}, s32[16,64]{1,0:T(8,128)}, u32[]{:S(2)}) copy-start(s32[16,64]{1,0:T(8,128)} %param.13) | copy-start | bytes 12292
  10.4 146.7 %all-gather.3.cloned.1.call-start = ((), (), s32[]{:S(2)}) async-start(), calls=%async_computation.4 | async-start | bytes 8650752 | tf_op jit(solution)/shard_map/all_gather | solution.py:46
  46.4 208.8 %all-gather.5.cloned.1.call-start = ((), (), s32[]{:S(2)}) async-start(), calls=%async_computation.5 | async-start | bytes 8650752 | tf_op jit(solution)/shard_map/all_gather | solution.py:47
  48.3 42.7 %all-to-all-start = ((bf16[8,32,2048]{2,0,1:T(8,128)(2,1)}), bf16[8,32,2048]{2,0,1:T(8,128)(2,1)S(1)}, u32[]{:S(2)}, u32[]{:S(2)}) async-start(bf16[8,32,2048]{2,0,1:T(8,128)(2,1)} %bitcast), calls=%async_computation | async-start | bytes 2097152 | tf_op jit(solution)/shard_map/all_to_all | solution.py:31
Sparse Core Ops, SparseCore 0:
  10.5 35.8 reduce-scatter.1
  49.0 107.9 all-gather.2
  159.6 95.5 all-gather.4
where the time goes:
time: 377 us; the launch traced here: 376 us
  waiting for transfers between devices  227 us (60%)
  matrix products  63 us (17%)
  blocking collectives  33.8 us (9%)
  local copies, waits for them, and re-layouts  17.6 us (5%)
  between operations  13.3 us (4%)
  other arithmetic  11.6 us (3%)
  starting transfers between devices  9.9 us (3%)
    all_gather x1, waiting for transfers between devices, local(): lax.all_gather(weights, 'mem', axis=0, tiled=True)  93.4 us
    all_gather x1, waiting for transfers between devices, local(): lax.all_gather(summed, 'mem', axis=0, tiled=True)  65 us
    dot_general x1, matrix products, from_moments(): jnp.einsum('bo,okl->bkl', coeff, moments, precision=high)  43.5 us
    reduce_scatter x1, waiting for transfers between devices, local(): lax.psum_scatter(partials[0].astype(jnp.bfloat16), 'vox', scatter_dimensi...  36 us
    all_to_all x1, blocking collectives, local(): lax.all_to_all(updated, 'mem', split_axis=0, concat_axis=1, tiled=True)  33.8 us
    all_to_all x1, waiting for transfers between devices, local(): lax.all_to_all(ensemble, 'mem', split_axis=1, concat_axis=0, tiled=True)  32.4 us
    dot_general x1, matrix products, block_moments(): jnp.einsum('kbi,lbi->bkl', obs_anom, weights, preferred_element_type=jnp....  17.8 us
    all_gather x1, local copies, waits for them, and re-layouts, local(): lax.all_gather(weights, 'mem', axis=0, tiled=True)  11.9 us
  transfers between devices with their start and end apart: 4, of which 4 were waited for; matrix products, arithmetic and copies ran while one was open for 2% of the time, Pallas kernels for 0%

commit v1 on v0

--- a/solution.py
+++ b/solution.py
@@ -4,6 +4,13 @@
 from jax.sharding import PartitionSpec as P
 
 OB = 128
+
+
+def refer_windows(v0):
+    return jnp.concatenate(
+        lax.all_to_all(jnp.stack(jnp.split(v0, lax.axis_size("mem"), axis=1), axis=0), "mem", 0, 0),
+        axis=0,
+    )
 
 
 def center(values):
@@ -28,7 +35,7 @@
     weights = (
         (observed[None, :] + perturb - summed.astype(jnp.float32)) / variance[None, :]
     ).astype(jnp.bfloat16)
-    members = lax.all_to_all(ensemble, "mem", split_axis=1, concat_axis=0, tiled=True)
+    members = refer_windows(ensemble)
     count = members.shape[0]
     blocks = obs_lists.shape[0]
     cells = members.shape[1] // blocks

time: 377 us -> 377 us (level)
  waiting for transfers between devices: 227 us -> 207 us
  local copies, waits for them, and re-layouts: 17.6 us -> 37.3 us
    unnamed x14 -> x47, local copies, waits for them, and re-layouts: 1.38 us -> 20.5 us
    all_gather x1, waiting for transfers between devices: 65 us -> 46.5 us  [local(): lax.all_gather(summed, 'mem', axis=0, tiled=True)]
  transfers between devices with their start and end apart: 4 -> 4, of which waited for: 4 -> 4; matrix products, arithmetic and copies ran while one was open for 2% -> 7% of each run, Pallas kernels for 0% -> 0%
where the time goes in v1:
time: 377 us; the launch traced here: 376 us
  waiting for transfers between devices  207 us (55%)
  matrix products  63.2 us (17%)
  local copies, waits for them, and re-layouts  37.3 us (10%)
  blocking collectives  33.8 us (9%)
  between operations  13.3 us (4%)
  other arithmetic  11.5 us (3%)
  starting transfers between devices  9.92 us (3%)
    all_gather x1, waiting for transfers between devices, local(): lax.all_gather(weights, 'mem', axis=0, tiled=True)  93.4 us
    all_gather x1, waiting for transfers between devices, local(): lax.all_gather(summed, 'mem', axis=0, tiled=True)  46.5 us
    dot_general x1, matrix products, from_moments(): jnp.einsum('bo,okl->bkl', coeff, moments, precision=high)  43.5 us
    reduce_scatter x1, waiting for transfers between devices, local(): lax.psum_scatter(partials[0].astype(jnp.bfloat16), 'vox', scatter_dimensi...  36 us
    all_to_all x1, blocking collectives, local(): lax.all_to_all(updated, 'mem', split_axis=0, concat_axis=1, tiled=True)  33.8 us
    all_to_all x1, waiting for transfers between devices, refer_windows(): lax.all_to_all(jnp.stack(jnp.split(v0, lax.axis_size('mem'), axis=1), axi...  31.3 us
    unnamed x47, local copies, waits for them, and re-layouts  20.5 us
    dot_general x1, matrix products, block_moments(): jnp.einsum('kbi,lbi->bkl', obs_anom, weights, preferred_element_type=jnp....  17.7 us
  transfers between devices with their start and end apart: 4, of which 4 were waited for; matrix products, arithmetic and copies ran while one was open for 7% of the time, Pallas kernels for 0%

profile of v1, /device:TPU:2, one launch (start us, length us, event | category | flops | bytes accessed | tf_op | source)
XLA Modules:
  0.0 376.3 jit_solution(1157940055044112627)
XLA Ops:
  6.5 0.0 reduce-scatter.2.cloned.1.call-start
  6.6 3.8 %convert_bitcast_fusion.1 = bf16[8,131072]{1,0:T(8,128)(2,1)} fusion(f32[1,8,131072]{2,1,0:T(8,128)} %param.9), kind=kLoop, calls=%fused_computation.18 | loop fusion | flops 1048576 | bytes 6291456 | tf_op jit(solution)/shard_map/convert_element_type | solution.py:33
  10.4 0.0 reduce-scatter.2.cloned.1.call-update
  10.5 0.0 all-gather.3.cloned.1.call-start
  10.5 36.0 %reduce-scatter.2.cloned.1.call-done = bf16[8,16384]{1,0:T(8,128)(2,1)} async-done(((bf16[8,131072]{1,0:T(8,128)(2,1)}), bf16[8,16384]{1,0:T(8,128)(2,1)}) %reduce-scatter.2.cloned.1.call-update) | async-done | bytes 262160 | tf_op jit(solution)/shard_map/reduce_scatter | solution.py:32
  46.5 0.0 all-gather.3.cloned.1.call-update
  46.5 0.0 all-gather.5.cloned.1.call-start
  46.6 0.0 copy-done
  46.6 0.6 constant_dynamic-update-slice_fusion.31
  47.2 0.6 constant_dynamic-update-slice_fusion.30
  47.8 0.6 constant_dynamic-update-slice_fusion.29
  48.4 0.6 constant_dynamic-update-slice_fusion.28
  49.0 0.0 copy-done.1
  49.1 0.0 copy-done.3
  49.1 0.0 copy-done.2
  49.1 1.8 divide_convert_fusion
  50.8 0.0 all-gather.5.cloned.1.call-update
  50.8 0.6 constant_dynamic-update-slice_fusion.27
  51.5 0.6 constant_dynamic-update-slice_fusion.26
  52.1 0.6 constant_dynamic-update-slice_fusion.25
  52.7 0.6 constant_dynamic-update-slice_fusion.24
  53.3 0.6 constant_dynamic-update-slice_fusion.23
  53.9 0.6 constant_dynamic-update-slice_fusion.22
  54.5 0.6 constant_dynamic-update-slice_fusion.21
  55.2 0.6 constant_dynamic-update-slice_fusion.20
  55.8 0.6 constant_dynamic-update-slice_fusion.19
  56.4 0.6 constant_dynamic-update-slice_fusion.18
  57.0 0.6 constant_dynamic-update-slice_fusion.17
  57.6 0.6 constant_dynamic-update-slice_fusion.16
  58.2 0.6 constant_dynamic-update-slice_fusion.15
  58.9 0.6 constant_dynamic-update-slice_fusion.14
  59.5 0.6 constant_dynamic-update-slice_fusion.13
  60.1 0.6 constant_dynamic-update-slice_fusion.12
  60.7 0.6 constant_dynamic-update-slice_fusion.11
  61.3 0.6 constant_dynamic-update-slice_fusion.10
  62.0 0.6 constant_dynamic-update-slice_fusion.9
  62.6 0.6 constant_dynamic-update-slice_fusion.8
  63.2 0.6 constant_dynamic-update-slice_fusion.7
  63.8 0.6 constant_dynamic-update-slice_fusion.6
  64.4 0.6 constant_dynamic-update-slice_fusion.5
  65.0 0.6 constant_dynamic-update-slice_fusion.4
  65.7 0.6 constant_dynamic-update-slice_fusion.3
  66.3 0.6 constant_dynamic-update-slice_fusion.2
  66.9 0.6 constant_dynamic-update-slice_fusion.1
  67.5 0.6 constant_dynamic-update-slice_fusion
  68.1 9.8 %all-to-all-start = ((bf16[32,8,2048]{2,1,0:T(8,128)(2,1)}), bf16[32,8,2048]{2,1,0:T(8,128)(2,1)S(1)}, u32[]{:S(2)}, u32[]{:S(2)}) async-start(bf16[32,8,2048]{2,1,0:T(8,128)(2,1)} %constant_dynamic-update-slice_fusion), calls=%async_computation | async-start | bytes 2097152 | tf_op jit(solution)/shard_map/all_to_all | solution.py:11
  78.0 0.1 select_reduce_fusion.1
  78.1 0.3 select_reduce_fusion
  78.4 31.3 %all-to-all-done = bf16[32,8,2048]{2,1,0:T(8,128)(2,1)S(1)} async-done(((bf16[32,8,2048]{2,1,0:T(8,128)(2,1)}), bf16[32,8,2048]{2,1,0:T(8,128)(2,1)S(1)}, u32[]{:S(2)}, u32[]{:S(2)}) %all-to-all-start) | async-done | bytes 1048608 | tf_op jit(solution)/shard_map/all_to_all | solution.py:11
  109.7 0.2 convert_bitcast_fusion
  110.0 0.4 copy.37
  110.4 0.2 convert_reduce_fusion.1
  110.6 46.5 %all-gather.3.cloned.1.call-done = bf16[256,16384]{1,0:T(8,128)(2,1)} async-done(((bf16[8,16384]{1,0:T(8,128)(2,1)}), bf16[256,16384]{1,0:T(8,128)(2,1)}) %all-gather.3.cloned.1.call-update) | async-done | bytes 8388624 | tf_op jit(solution)/shard_map/all_gather | solution.py:53
  157.1 4.8 %convert_reduce_fusion = f32[16384]{0:T(1024)S(1)} fusion(bf16[256,16384]{1,0:T(8,128)(2,1)} %all-gather.3.cloned.1.call-done), kind=kLoop, calls=%fused_computation.3 | loop fusion | flops 8372224 | bytes 8454144 | tf_op jit(solution)/shard_map/reduce_sum | solution.py:18
  161.9 93.4 %all-gather.5.cloned.1.call-done = bf16[256,16384]{1,0:T(8,128)(2,1)} async-done(((bf16[8,16384]{1,0:T(8,128)(2,1)}), bf16[256,16384]{1,0:T(8,128)(2,1)}) %all-gather.5.cloned.1.call-update) | async-done | bytes 8388624 | tf_op jit(solution)/shard_map/all_gather | solution.py:54
  255.3 11.9 %copy.28 = bf16[256,16384]{0,1:T(8,128)(2,1)} copy(bf16[256,16384]{1,0:T(8,128)(2,1)} %all-gather.5.cloned.1.call-done) | data formatting | bytes 16777216 | tf_op jit(solution)/shard_map/all_gather | solution.py:54
  267.2 17.7 %fusion.4 = f32[128,256,256]{2,1,0:T(8,128)} fusion(bf16[256,128,128]{0,2,1:T(8,128)(2,1)} %bitcast.89, bf16[256,16384]{1,0:T(8,128)(2,1)} %all-gather.3.cloned.1.call-done, f32[16384]{0:T(1024)S(1)} %broadcast_multiply_fusion), kind=kOutput, calls=%fused_computation.6 | convolution fusion | flops 2160066560 | bytes 50397184 | tf_op jit(solution)/shard_map/kbi,lbi->bkl/dot_general | solution.py:22
  284.9 43.5 %fusion.11 = bf16[16,256,256]{2,0,1:T(8,128)(2,1)S(1)} fusion(f32[128,256,256]{2,1,0:T(8,128)} %fusion.4, f32[16,128]{1,0:T(8,128)S(1)} %select_reduce_fusion), kind=kOutput, calls=%fused_computation.19 | convolution fusion | flops 1611661312 | bytes 35659776 | tf_op jit(solution)/shard_map/bo,okl->bkl/dot_general | solution.py:27
  328.5 2.0 multiply_bitcast_fusion
  330.5 2.5 copy.34
  333.0 1.7 mul.36
  334.7 0.3 fusion.7
  335.0 33.8 %all_to_all.21 = bf16[32,8,2048]{2,1,0:T(8,128)(2,1)S(1)} all-to-all(bf16[32,8,2048]{2,1,0:T(8,128)(2,1)S(1)} %fusion.7), channel_id=1, replica_groups=mesh['vox'=8,'mem'=32] {'mem'}, dimensions={0} | all-to-all | bytes 2097152 | tf_op jit(solution)/shard_map/all_to_all | solution.py:60
  368.8 1.0 copy.86
  (12 shorter events, 0.0 us)
Async XLA Ops:
  6.5 40.0 %copy-start = (bf16[8,65536]{1,0:T(8,128)(2,1)S(1)}, bf16[8,65536]{1,0:T(8,128)(2,1)}, u32[]{:S(2)}) copy-start(bf16[8,65536]{1,0:T(8,128)(2,1)} %param.8) | copy-start | bytes 3145732
  6.5 42.5 %copy-start.1 = (f32[8,16384]{1,0:T(8,128)S(1)}, f32[8,16384]{1,0:T(8,128)}, u32[]{:S(2)}) copy-start(f32[8,16384]{1,0:T(8,128)} %param.10) | copy-start | bytes 1572868
  6.5 42.5 %copy-start.3 = (f32[16384]{0:T(1024)S(1)}, f32[16384]{0:T(1024)}, u32[]{:S(2)}) copy-start(f32[16384]{0:T(1024)} %param.11) | copy-start | bytes 196612
  6.5 42.5 %copy-start.2 = (f32[16384]{0:T(1024)S(1)}, f32[16384]{0:T(1024)}, u32[]{:S(2)}) copy-start(f32[16384]{0:T(1024)} %param.12) | copy-start | bytes 196612
  6.5 40.0 %reduce-scatter.2.cloned.1.call-start = ((), (), s32[]{:S(2)}) async-start(), calls=%async_computation.3 | async-start | bytes 2359296 | tf_op jit(solution)/shard_map/reduce_scatter | solution.py:32
  10.4 67.5 %copy-start.5 = (s32[16,64]{1,0:T(8,128)S(1)}, s32[16,64]{1,0:T(8,128)}, u32[]{:S(2)}) copy-start(s32[16,64]{1,0:T(8,128)} %param.14) | copy-start | bytes 12292
  10.4 67.5 %copy-start.6 = (f32[16]{0:T(128)S(1)}, f32[16]{0:T(128)}, u32[]{:S(2)}) copy-start(f32[16]{0:T(128)} %param.15) | copy-start | bytes 196
  10.4 67.6 %copy-start.4 = (s32[16,64]{1,0:T(8,128)S(1)}, s32[16,64]{1,0:T(8,128)}, u32[]{:S(2)}) copy-start(s32[16,64]{1,0:T(8,128)} %param.13) | copy-start | bytes 12292
  10.5 146.6 %all-gather.3.cloned.1.call-start = ((), (), s32[]{:S(2)}) async-start(), calls=%async_computation.4 | async-start | bytes 8650752 | tf_op jit(solution)/shard_map/all_gather | solution.py:53
  46.5 208.8 %all-gather.5.cloned.1.call-start = ((), (), s32[]{:S(2)}) async-start(), calls=%async_computation.5 | async-start | bytes 8650752 | tf_op jit(solution)/shard_map/all_gather | solution.py:54
  68.1 41.6 %all-to-all-start = ((bf16[32,8,2048]{2,1,0:T(8,128)(2,1)}), bf16[32,8,2048]{2,1,0:T(8,128)(2,1)S(1)}, u32[]{:S(2)}, u32[]{:S(2)}) async-start(bf16[32,8,2048]{2,1,0:T(8,128)(2,1)} %constant_dynamic-update-slice_fusion), calls=%async_computation | async-start | bytes 2097152 | tf_op jit(solution)/shard_map/all_to_all | solution.py:11
Sparse Core Ops, SparseCore 0:
  10.6 35.8 reduce-scatter.1
  49.1 107.9 all-gather.2
  159.7 95.5 all-gather.4
